TPU v7x, 32 devices: a whole 2x2x4 slice. The times are simulated.
32 devices in a mesh: rows: 8 (over y, x, core), chip: 4 (over z).
Axes of the slice: x: 2, y: 2, z: 4, core: 2. Of those that a mesh axis runs over, the one named last changes fastest.
Arguments:
- spectra: float32 [8192, 512], P(('rows', 'chip')), may hold values from -250 to 250
Outputs:
- whitened: float32 [8192, 512], P(('rows', 'chip'))
- triangle: float32 [512, 512], replicated
All inputs are finite; a program needn't handle non-finite values.
Results may differ from a plain program's by a relative error of at most 0.000055.
Values sent between devices are 32-bit elements; how exact they have to be, the bound alone decides.
A program may use at most 64 MiB of HBM per device.

v0:
```python
import math

import jax
import jax.numpy as jnp
from jax import lax
from jax.sharding import PartitionSpec as P


def summed_gram(block):
    gram = lax.dot_general(
        block,
        block,
        (((0,), (0,)), ((), ())),
        precision=lax.Precision.HIGHEST,
        preferred_element_type=jnp.float32,
    )
    band = lax.psum_scatter(gram, "rows", scatter_dimension=0, tiled=True)
    band = lax.psum(band, "chip")
    return lax.all_gather(band, "rows", axis=0, tiled=True)


def on_device(spectra):
    total_rows = lax.axis_size("rows") * lax.axis_size("chip") * spectra.shape[0]
    lower = jnp.linalg.cholesky(summed_gram(spectra))
    basis = lax.linalg.triangular_solve(
        lower, spectra, left_side=False, lower=True, transpose_a=True
    )
    factor_scale = math.sqrt(total_rows)
    return (basis * factor_scale, lower.T / factor_scale)


def solution(mesh):
    return jax.shard_map(
        on_device,
        mesh=mesh,
        in_specs=(P(("rows", "chip"), None),),
        out_specs=(P(("rows", "chip"), None), P()),
        check_vma=False,
    )
```

profile of v0, /device:TPU:0, one launch (start us, length us, event | category | flops | bytes accessed | tf_op | source)
XLA Modules:
  0.0 267.2 jit_solution(14837119055252638313)
XLA Ops:
  7.2 0.0 reduce-scatter.4.cloned.1.call-start
  7.2 3.3 %fusion.32 = f32[512,512]{1,0:T(8,128)} fusion(f32[256,512]{1,0:T(8,128)} %param.1), kind=kOutput, calls=%fused_computation.69 | convolution fusion | flops 805306368 | bytes 1572864
  10.5 0.0 reduce-scatter.4.cloned.1.call-update
  10.5 0.0 all-reduce.3.cloned.1.call-start
  10.6 39.9 %reduce-scatter.4.cloned.1.call-done = f32[64,512]{1,0:T(8,128)} async-done(((f32[512,512]{1,0:T(8,128)}), f32[64,512]{1,0:T(8,128)}) %reduce-scatter.4.cloned.1.call-update) | async-done | bytes 131088
  50.5 1.7 copy.14
  52.2 0.0 all-reduce.3.cloned.1.call-update
  52.3 0.0 all-gather.2.cloned.1.call-start
  52.3 36.4 %all-reduce.3.cloned.1.call-done = f32[64,512]{0,1:T(8,128)} async-done(((f32[64,512]{0,1:T(8,128)}), f32[64,512]{0,1:T(8,128)}) %all-reduce.3.cloned.1.call-update) | async-done | bytes 131088 | tf_op jit(solution)/shard_map/psum | solution.py:18
  88.7 1.7 copy.8
  90.4 0.0 all-gather.2.cloned.1.call-update
  90.5 24.1 %all-gather.2.cloned.1.call-done = f32[512,512]{1,0:T(8,128)} async-done(((f32[64,512]{1,0:T(8,128)}), f32[512,512]{1,0:T(8,128)}) %all-gather.2.cloned.1.call-update) | async-done | bytes 1048592 | tf_op jit(solution)/shard_map/all_gather | solution.py:19
  114.6 0.0 copy-start.1
  114.6 1.6 copy.9
  116.3 0.0 copy-done.1
  116.3 0.2 fusion
  116.5 11.7 %cholesky.104 = f32[128,128]{1,0:T(8,128)S(1)} custom-call(f32[128,128]{1,0:T(8,128)S(1)} %cholesky.266), custom_call_target="Cholesky" | custom-call | tf_op jit(solution)/shard_map/jit(cholesky)/cholesky | solution.py:24
  128.3 9.8 %custom-call.30 = f32[1,128,128]{1,2,0:T(8,128)S(1)} custom-call(f32[1,128,128]{2,1,0:T(8,128)S(1)} %get-tuple-element.35), custom_call_target="InvertDiagBlocksLowerTriangular" | custom-call | tf_op jit(solution)/shard_map/jit(cholesky)/cholesky | solution.py:24
  138.1 0.1 cholesky.224
  138.2 0.3 constant_dynamic-update-slice_fusion.3
  138.5 0.3 convolution_subtract_fusion
  138.9 11.7 %cholesky.217 = f32[128,128]{1,0:T(8,128)S(1)} custom-call(f32[128,128]{1,0:T(8,128)S(1)} %cholesky.270), custom_call_target="Cholesky" | custom-call | tf_op jit(solution)/shard_map/jit(cholesky)/cholesky | solution.py:24
  150.6 9.9 %custom-call.31 = f32[1,128,128]{1,2,0:T(8,128)S(1)} custom-call(f32[1,128,128]{2,1,0:T(8,128)S(1)} %get-tuple-element.32), custom_call_target="InvertDiagBlocksLowerTriangular" | custom-call | tf_op jit(solution)/shard_map/jit(cholesky)/cholesky | solution.py:24
  160.6 0.3 convolution_dynamic-update-slice_fusion
  160.9 0.4 convolution_subtract_fusion.3
  161.3 11.7 %cholesky.238 = f32[128,128]{1,0:T(8,128)S(1)} custom-call(f32[128,128]{1,0:T(8,128)S(1)} %cholesky.275), custom_call_target="Cholesky" | custom-call | tf_op jit(solution)/shard_map/jit(cholesky)/cholesky | solution.py:24
  173.0 0.7 compare_reduce_fusion.1
  173.7 9.8 %custom-call.32 = f32[1,128,128]{1,2,0:T(8,128)S(1)} custom-call(f32[1,128,128]{2,1,0:T(8,128)S(1)} %get-tuple-element.29), custom_call_target="InvertDiagBlocksLowerTriangular" | custom-call | tf_op jit(solution)/shard_map/jit(cholesky)/cholesky | solution.py:24
  183.5 0.2 convolution_dynamic-update-slice_fusion.1
  183.8 0.4 convolution_subtract_fusion.5
  184.1 11.7 %cholesky.255 = f32[128,128]{1,0:T(8,128)S(1)} custom-call(f32[128,128]{1,0:T(8,128)S(1)} %convolution_subtract_fusion.5), custom_call_target="Cholesky" | custom-call | tf_op jit(solution)/shard_map/jit(cholesky)/cholesky | solution.py:24
  195.9 0.6 compare_reduce_fusion
  196.5 0.9 compare_reduce_fusion.2
  199.9 0.0 copy-start
  199.9 1.2 multiply_bitcast_fusion
  201.2 12.0 %while.1 = (s32[]{:T(128)}, f32[512,512]{1,0:T(8,128)}, s32[4,2]{0,1:T(2,128)S(1)}, f32[4,128,128]{2,1,0:T(8,128)S(1)}, s32[]{:T(128)}) while((s32[]{:T(128)}, f32[512,512]{1,0:T(8,128)}, s32[4,2]{0,1:T(2,128)S(1)}, f32[4,128,128]{2,1,0:T(8,128)S(1)}, s32[]{:T(128)}) %tuple.34), condition=%wide.while_cond, body=%wide.while_body.sunk | while | flops 2 | bytes 131181 | solution.py:25
  201.2 0.1 constant_dynamic-slice_fusion.2
  201.3 0.6 fusion.41
  201.9 2.3 bitcast_dynamic-update-slice_fusion.2
  204.2 0.1 constant_dynamic-slice_fusion.2
  204.3 0.6 fusion.41
  204.9 2.3 bitcast_dynamic-update-slice_fusion.2
  207.2 0.1 constant_dynamic-slice_fusion.2
  207.3 0.6 fusion.41
  207.9 2.3 bitcast_dynamic-update-slice_fusion.2
  210.3 0.1 constant_dynamic-slice_fusion.2
  210.3 0.6 fusion.41
  210.9 2.3 bitcast_dynamic-update-slice_fusion.2
  213.2 39.3 %custom-call.33 = f32[4,128,128]{1,2,0:T(8,128)S(1)} custom-call(f32[4,128,128]{2,1,0:T(8,128)S(1)} %get-tuple-element.9), custom_call_target="InvertDiagBlocksLowerTriangular" | custom-call | tf_op jit(solution)/shard_map/triangular_solve | solution.py:25
  252.5 0.0 copy-done
  252.6 0.3 fusion.18
  252.9 1.2 convolution_subtract_fusion.4
  254.1 0.3 fusion.22
  254.4 1.5 convolution_subtract_fusion.2
  255.9 0.3 fusion.21
  256.3 1.8 convolution_subtract_fusion.1
  258.0 0.3 fusion.20
  258.4 1.0 copy.10
  259.4 1.3 copy.11
  (11 shorter events, 0.2 us)
Async XLA Ops:
  7.2 43.3 %reduce-scatter.4.cloned.1.call-start = ((), (), s32[]{:S(2)}) async-start(), calls=%async_computation.3 | async-start | bytes 1179648
  10.5 78.2 %all-reduce.3.cloned.1.call-start = ((), (), s32[]{:S(2)}) async-start(), calls=%async_computation.1 | async-start | bytes 524288 | tf_op jit(solution)/shard_map/psum | solution.py:18
  52.3 62.4 %all-gather.2.cloned.1.call-start = ((), (), s32[]{:S(2)}) async-start(), calls=%async_computation.2 | async-start | bytes 1179648 | tf_op jit(solution)/shard_map/all_gather | solution.py:19
  114.6 1.7 copy-start.1
  199.9 52.6 %copy-start = (f32[256,512]{1,0:T(8,128)S(1)}, f32[256,512]{1,0:T(8,128)}, u32[]{:S(2)}) copy-start(f32[256,512]{1,0:T(8,128)} %param.1) | copy-start | bytes 1572868
Sparse Core Ops, SparseCore 0:
  11.7 38.6 reduce-scatter.3
  53.4 35.2 all-reduce.2
  91.4 23.2 all-gather.1
where the time goes:
time: 268 us; the launch traced here: 267 us
  other arithmetic  120 us (45%)
  waiting for transfers between devices  101 us (38%)
  local copies, waits for them, and re-layouts  19.5 us (7%)
  between operations  16.5 us (6%)
  matrix products  10.9 us (4%)
    another operation x14, other arithmetic, on_device(): lower = jnp.linalg.cholesky(summed_gram(spectra))  78.8 us
    unnamed x4, waiting for transfers between devices  40 us
    another operation x2, other arithmetic, on_device(): lax.linalg.triangular_solve(lower, spectra, left_side=False, lower=True,...  39.3 us
    psum x1, waiting for transfers between devices, summed_gram(): band = lax.psum(band, 'chip')  36.4 us
    all_gather x1, waiting for transfers between devices, summed_gram(): return lax.all_gather(band, 'rows', axis=0, tiled=True)  24.1 us
    another operation x12, local copies, waits for them, and re-layouts  12 us
    another operation x7, matrix products, on_device(): lax.linalg.triangular_solve(lower, spectra, left_side=False, lower=True,...  5.73 us
  transfers between devices with their start and end apart: 3, of which 3 were waited for; matrix products, arithmetic and copies ran while one was open for 0% of the time, Pallas kernels for 0%

commit v1 on v0

v1 whole, which is shorter than its diff:
```python
import functools
import math

import jax
import jax.numpy as jnp
from jax import lax
from jax.experimental import pallas as pl
from jax.experimental.pallas import tpu as pltpu
from jax.sharding import PartitionSpec as P

WIDE = 128
SUB = 8
HIGHEST = lax.Precision.HIGHEST


def mm(a, b, dims):
    return lax.dot_general(
        a, b, (dims, ((), ())), precision=HIGHEST, preferred_element_type=jnp.float32
    )


def row_of(x, k):
    return jnp.broadcast_to(x[k : k + 1, :], (SUB, WIDE))


def lane_of(x, k):
    return jnp.broadcast_to(x[:, k : k + 1], (SUB, WIDE))


def factor_block(groups):
    count = len(groups)
    groups = list(groups)
    sub = lax.broadcasted_iota(jnp.int32, (SUB, WIDE), 0)
    lane = lax.broadcasted_iota(jnp.int32, (SUB, WIDE), 1)
    upper, inverse = [], []
    diag = [lane_of(groups[0], k) for k in range(SUB)]
    for g in range(count):
        p0 = g * SUB
        more = g + 1 < count
        own = (lane >= p0) & (lane < p0 + SUB)
        plain = groups[g]
        both = jnp.where(own, jnp.where(lane - p0 == sub, 1.0, 0.0), plain)
        full = both
        low = list(diag)
        jordan = list(diag)
        if more:
            after = [lane_of(groups[g + 1], p0 + k) for k in range(SUB)]
            ahead = [lane_of(groups[g + 1], p0 + SUB + k) for k in range(SUB)]
            after_low = list(after)
        for k in range(SUB):
            scale = lax.rsqrt(row_of(low[k], k))
            low_k = low[k] * scale
            times = [None] * SUB
            for j in range(k + 1, SUB):
                times[j] = row_of(low[j], k) * scale
            for j in range(k + 1, SUB):
                low[j] = low[j] - low_k * times[j]
            if more:
                after_k = after_low[k] * scale
                for j in range(k + 1, SUB):
                    after_low[j] = after_low[j] - after_k * times[j]
                for j in range(SUB):
                    ahead[j] = ahead[j] - after_k * row_of(after_k, j)
            below = jnp.where(sub > k, low_k, 0.0)
            at = sub == k
            plain_k = row_of(plain, k) * scale
            plain = jnp.where(at, plain_k, plain - below * plain_k)
            both_k = row_of(both, k) * scale
            both = jnp.where(at, both_k, both - below * both_k)
            if more:
                square = scale * scale
                full_k = row_of(full, k) * square
                full = jnp.where(at, full_k, full - jordan[k] * full_k)
                for j in range(k + 1, SUB):
                    t = row_of(jordan[j], k) * square
                    jordan[j] = jnp.where(at, t, jordan[j] - jordan[k] * t)
        upper.append(jnp.where(lane >= p0 + sub, jnp.where(own, plain, both), 0.0))
        inverse.append(jnp.where(lane <= p0 + sub, both, 0.0))
        if more:
            rows = [row_of(full, k) for k in range(SUB)]
            for q in range(g + 1, count):
                old = groups[q]
                new = jnp.where(own, 0.0, old)
                for k in range(SUB):
                    column = after[k] if q == g + 1 else lane_of(old, p0 + k)
                    new = new - column * rows[k]
                groups[q] = new
            diag = ahead
    return upper, inverse


def factor_kernel(row_scale, gram, spectra, whitened, triangle, work, held):
    n = gram.shape[0]
    blocks = n // WIDE
    groups = WIDE // SUB

    def at(i):
        return pl.ds(i * WIDE, WIDE)

    for p in range(blocks):
        source = gram if p == 0 else work
        rows = [
            source[p * WIDE + g * SUB : p * WIDE + (g + 1) * SUB, p * WIDE : (p + 1) * WIDE]
            for g in range(groups)
        ]
        upper, inverse = factor_block(rows)
        upper = jnp.concatenate(upper, axis=0)
        inverse = jnp.concatenate(inverse, axis=0)
        triangle[at(p), at(p)] = upper * (1.0 / row_scale)
        for q in range(p):
            triangle[at(p), at(q)] = jnp.zeros((WIDE, WIDE), jnp.float32)
        right = []
        for q in range(p + 1, blocks):
            block = mm(inverse, source[at(p), at(q)], ((1,), (0,)))
            right.append(block)
            triangle[at(p), at(q)] = block * (1.0 / row_scale)
            if q == p + 1:
                work[at(q), at(q)] = source[at(q), at(q)] - mm(block, block, ((0,), (0,)))
        for i, q in enumerate(range(p + 1, blocks)):
            for j, r in enumerate(range(p + 1, blocks)):
                if r < q or (q == p + 1 and r == q):
                    continue
                work[at(q), at(r)] = source[at(q), at(r)] - mm(right[i], right[j], ((0,), (0,)))
        slab = spectra if p == 0 else held
        basis = mm(slab[:, at(p)], inverse, ((1,), (1,)))
        whitened[:, at(p)] = basis * row_scale
        for i, q in enumerate(range(p + 1, blocks)):
            held[:, at(q)] = slab[:, at(q)] - mm(basis, right[i], ((1,), (0,)))


def factor(gram, spectra, total_rows):
    n = gram.shape[0]
    return pl.pallas_call(
        functools.partial(factor_kernel, math.sqrt(total_rows)),
        out_shape=(
            jax.ShapeDtypeStruct(spectra.shape, jnp.float32),
            jax.ShapeDtypeStruct((n, n), jnp.float32),
        ),
        in_specs=[pl.BlockSpec(memory_space=pltpu.VMEM)] * 2,
        out_specs=(pl.BlockSpec(memory_space=pltpu.VMEM),) * 2,
        scratch_shapes=[
            pltpu.VMEM((n, n), jnp.float32),
            pltpu.VMEM(spectra.shape, jnp.float32),
        ],
        compiler_params=pltpu.CompilerParams(vmem_limit_bytes=40 * 2**20),
    )(gram, spectra)


def summed_gram(block):
    gram = mm(block, block, ((0,), (0,)))
    band = lax.psum_scatter(gram, "rows", scatter_dimension=0, tiled=True)
    band = lax.psum(band, "chip")
    return lax.all_gather(band, "rows", axis=0, tiled=True)


def on_device(spectra):
    total_rows = lax.axis_size("rows") * lax.axis_size("chip") * spectra.shape[0]
    return factor(summed_gram(spectra), spectra, total_rows)


def solution(mesh):
    return jax.shard_map(
        on_device,
        mesh=mesh,
        in_specs=(P(("rows", "chip"), None),),
        out_specs=(P(("rows", "chip"), None), P()),
        check_vma=False,
    )
```

time: 268 us -> 133 us (0.50)
  other arithmetic: 120 us -> 0 us
  local copies, waits for them, and re-layouts: 19.5 us -> 1.23 us
  Pallas kernels: 0 us -> 12.9 us
  matrix products: 10.9 us -> 3.2 us
  between operations: 16.5 us -> 13.7 us
    another operation x16 -> x0, other arithmetic: 118 us -> none  [the longest x14 78.8 us: on_device(): lower = jnp.linalg.cholesky(summed_gram(spectra))]
    reduce_scatter x0 -> x1, waiting for transfers between devices: none -> 40 us  [summed_gram(): band = lax.psum_scatter(gram, 'rows', scatter_dimension=0, tiled=True)]
    unnamed x4 -> x3, waiting for transfers between devices: 40 us -> 0.05 us
    pallas_call x0 -> x1, Pallas kernels: none -> 12.9 us  [factor(): pl.pallas_call(functools.partial(factor_kernel, math.sqrt(total_rows)), o...]
    another operation x17 -> x0, local copies, waits for them, and re-layouts: 12.1 us -> none
    another operation x13 -> x0, matrix products: 7.6 us -> none  [the longest x7 5.73 us: on_device(): lax.linalg.triangular_solve(lower, spectra, left_side=False, lower=True,...]
    unnamed x1 -> x0, matrix products: 3.3 us -> none
    dot_general x0 -> x1, matrix products: none -> 3.2 us  [mm(): lax.dot_general(a, b, (dims, ((), ())), precision=HIGHEST, preferred_elem...]
where the time goes in v1:
time: 133 us
  waiting for transfers between devices  102 us (77%)
  between operations  13.7 us (10%)
  Pallas kernels  12.9 us (10%)
  matrix products  3.2 us (2%)
    reduce_scatter x1, waiting for transfers between devices, summed_gram(): band = lax.psum_scatter(gram, 'rows', scatter_dimension=0, tiled=True)  40 us
    psum x1, waiting for transfers between devices, summed_gram(): band = lax.psum(band, 'chip')  36.7 us
    all_gather x1, waiting for transfers between devices, summed_gram(): return lax.all_gather(band, 'rows', axis=0, tiled=True)  25.2 us
    pallas_call x1, Pallas kernels, factor(): pl.pallas_call(functools.partial(factor_kernel, math.sqrt(total_rows)), o...  12.9 us
    dot_general x1, matrix products, mm(): lax.dot_general(a, b, (dims, ((), ())), precision=HIGHEST, preferred_elem...  3.2 us
  transfers between devices with their start and end apart: 3, of which 3 were waited for; matrix products, arithmetic and copies ran while one was open for 0% of the time, Pallas kernels for 0%

profile of v1, /device:TPU:0, one launch (start us, length us, event | category | flops | bytes accessed | tf_op | source)
XLA Modules:
  0.0 133.2 jit_solution(5777952995400690775)
XLA Ops:
  7.2 0.0 reduce-scatter.2.cloned.1.call-start
  7.2 3.2 %fusion = f32[512,512]{1,0:T(8,128)} fusion(f32[256,512]{1,0:T(8,128)} %spectra.1), kind=kOutput, calls=%fused_computation | convolution fusion | flops 805306368 | bytes 1572864 | tf_op jit(solution)/shard_map/dot_general | solution.py:17
  10.4 0.0 copy-start
  10.4 0.0 reduce-scatter.2.cloned.1.call-update
  10.4 0.0 all-reduce.2.cloned.1.call-start
  10.5 40.0 %reduce-scatter.2.cloned.1.call-done = f32[64,512]{1,0:T(8,128)} async-done(((f32[512,512]{1,0:T(8,128)}), f32[64,512]{1,0:T(8,128)}) %reduce-scatter.2.cloned.1.call-update) | async-done | bytes 131088 | tf_op jit(solution)/shard_map/reduce_scatter | solution.py:151
  50.5 0.0 all-reduce.2.cloned.1.call-update
  50.5 0.0 all-gather.2.cloned.1.call-start
  50.6 36.7 %all-reduce.2.cloned.1.call-done = f32[64,512]{1,0:T(8,128)} async-done(((f32[64,512]{1,0:T(8,128)}), f32[64,512]{1,0:T(8,128)}) %all-reduce.2.cloned.1.call-update) | async-done | bytes 131088 | tf_op jit(solution)/shard_map/psum | solution.py:152
  87.3 0.0 all-gather.2.cloned.1.call-update
  87.3 25.2 %all-gather.2.cloned.1.call-done.gram = f32[512,512]{1,0:T(8,128)} async-done(((f32[64,512]{1,0:T(8,128)}), f32[512,512]{1,0:T(8,128)}) %all-gather.2.cloned.1.call-update) | async-done | bytes 1048592 | tf_op jit(solution)/shard_map/all_gather | solution.py:153
  112.5 0.0 copy-done
  112.5 0.0 copy-start.1
  112.5 1.2 copy-done.1
  113.7 12.9 %shard_map.30 = (f32[256,512]{1,0:T(8,128)}, f32[512,512]{1,0:T(8,128)}) custom-call(f32[512,512]{1,0:T(8,128)S(1)} %copy-done.1, f32[256,512]{1,0:T(8,128)S(1)} %copy-done), custom_call_target="tpu_custom_call" | custom-call | tf_op jit(solution)/shard_map/pallas_call | solution.py:133
Async XLA Ops:
  7.2 43.3 %reduce-scatter.2.cloned.1.call-start = ((), (), s32[]{:S(2)}) async-start(), calls=%async_computation.1 | async-start | bytes 1179648 | tf_op jit(solution)/shard_map/reduce_scatter | solution.py:151
  10.4 102.1 %copy-start = (f32[256,512]{1,0:T(8,128)S(1)}, f32[256,512]{1,0:T(8,128)}, u32[]{:S(2)}) copy-start(f32[256,512]{1,0:T(8,128)} %spectra.1) | copy-start | bytes 1572868
  10.4 76.8 %all-reduce.2.cloned.1.call-start = ((), (), s32[]{:S(2)}) async-start(), calls=%async_computation.2 | async-start | bytes 262144 | tf_op jit(solution)/shard_map/psum | solution.py:152
  50.5 62.0 %all-gather.2.cloned.1.call-start = ((), (), s32[]{:S(2)}) async-start(), calls=%async_computation.3 | async-start | bytes 1179648 | tf_op jit(solution)/shard_map/all_gather | solution.py:153
  112.5 1.2 copy-start.1
Sparse Core Ops, SparseCore 0:
  11.7 38.7 reduce-scatter.1
  52.8 34.4 all-reduce.1
  89.3 23.1 all-gather.1

commit v2 on v1

--- a/solution.py
+++ b/solution.py
@@ -89,20 +89,190 @@
     return upper, inverse
 
 
+def block_pairs(blocks):
+    return [(i, j) for i in range(blocks) for j in range(i, blocks)]
+
+
+def gram_kernel(sizes, spectra, out, packed, from_pair, halves, from_hi, sums, from_chip, *sems):
+    pairs_n, chips, piece = sizes
+    send_a, recv_a, send_b, recv_b, send_c, recv_c = sems[:6]
+    send_gc, recv_gc, send_gb, recv_gb, send_ga, recv_ga, gathered = sems[6:]
+    part = chips * piece
+    half = pairs_n * part
+    row, chip = lax.axis_index("rows"), lax.axis_index("chip")
+    hi, lo = row // 2, row % 2
+    other = (hi * 2 + 1 - lo, chip)
+
+    def hi_at(d):
+        return lax.rem(hi + d, pairs_n)
+
+    def chip_at(d):
+        return lax.rem(chip + d, chips)
+
+    def hi_device(d):
+        return (hi_at(d) * 2 + lo, chip)
+
+    def chip_device(d):
+        return (row, chip_at(d))
+
+    def remote(src, dst, send, recv, device):
+        return pltpu.make_async_remote_copy(
+            src_ref=src, dst_ref=dst, send_sem=send, recv_sem=recv,
+            device_id=device, device_id_type=pl.DeviceIdType.MESH,
+        )
+
+    barrier = pltpu.get_barrier_semaphore()
+    partners = [other]
+    partners += [hi_device(d) for d in range(1, pairs_n)]
+    partners += [chip_device(d) for d in range(1, chips)]
+    for device in partners:
+        pl.semaphore_signal(barrier, inc=1, device_id=device, device_id_type=pl.DeviceIdType.MESH)
+
+    n = spectra.shape[1]
+    tiles = WIDE // SUB
+    used = 0
+    for i, j in block_pairs(n // WIDE):
+        left = spectra[:, i * WIDE : (i + 1) * WIDE]
+        right = spectra[:, j * WIDE : (j + 1) * WIDE]
+        packed[used : used + tiles] = mm(left, right, ((0,), (0,))).reshape(tiles, SUB, WIDE)
+        used += tiles
+    if used < packed.shape[0]:
+        packed[used:] = jnp.zeros((packed.shape[0] - used, SUB, WIDE), jnp.float32)
+    pl.semaphore_wait(barrier, len(partners))
+
+    started = []
+    order = list(range(1, pairs_n)) + [0]
+    pair_copies = {}
+    for d in order:
+        at = hi_at(d) * part
+        copy = remote(
+            packed.at[pl.ds((1 - lo) * half + at, part)], from_pair.at[d],
+            send_a.at[d], recv_a.at[d], other,
+        )
+        copy.start()
+        pair_copies[d] = copy
+        started.append(copy)
+    hi_copies = []
+    for d in order:
+        pair_copies[d].wait_recv()
+        mine = packed[pl.ds(lo * half + hi_at(d) * part, part)] + from_pair[d]
+        halves[d] = mine
+        if d:
+            copy = remote(halves.at[d], from_hi.at[d], send_b.at[d], recv_b.at[d], hi_device(d))
+            copy.start()
+            hi_copies.append(copy)
+            started.append(copy)
+    for copy in hi_copies:
+        copy.wait_recv()
+    chip_copies = []
+    for d in list(range(1, chips)) + [0]:
+        at = pl.ds(chip_at(d) * piece, piece)
+        mine = halves[0, at]
+        for e in range(1, pairs_n):
+            mine = mine + from_hi[e, at]
+        sums[d] = mine
+        if d:
+            copy = remote(sums.at[d], from_chip.at[d], send_c.at[d], recv_c.at[d], chip_device(d))
+            copy.start()
+            chip_copies.append(copy)
+            started.append(copy)
+    total = sums[0]
+    for d, copy in enumerate(chip_copies, 1):
+        copy.wait_recv()
+        total = total + from_chip[d]
+
+    own = (lo * pairs_n + hi) * part
+    spot = gathered.at[pl.ds(own + chip * piece, piece)]
+    gathered[pl.ds(own + chip * piece, piece)] = total
+    gather_chip = []
+    for d in range(1, chips):
+        copy = remote(spot, spot, send_gc.at[d], recv_gc.at[d], chip_device(d))
+        copy.start()
+        gather_chip.append(copy)
+    for copy in gather_chip:
+        copy.wait_recv()
+    started += gather_chip
+    gather_hi = []
+    spot = gathered.at[pl.ds(own, part)]
+    for d in range(1, pairs_n):
+        copy = remote(spot, spot, send_gb.at[d], recv_gb.at[d], hi_device(d))
+        copy.start()
+        gather_hi.append(copy)
+    started += gather_hi
+    gather_pair = []
+    for d in range(pairs_n):
+        source = lax.rem(hi + pairs_n - d, pairs_n)
+        spot = gathered.at[pl.ds((lo * pairs_n + source) * part, part)]
+        if d:
+            gather_hi[d - 1].wait_recv()
+        copy = remote(spot, spot, send_ga.at[d], recv_ga.at[d], other)
+        copy.start()
+        gather_pair.append(copy)
+    for copy in gather_pair:
+        copy.wait_recv()
+    started += gather_pair
+    out[...] = gathered[...]
+    for copy in started:
+        copy.wait_send()
+
+
+def summed_gram(spectra):
+    rows, chips = lax.axis_size("rows"), lax.axis_size("chip")
+    pairs_n = rows // 2
+    n = spectra.shape[1]
+    used = len(block_pairs(n // WIDE)) * (WIDE // SUB)
+    piece = -(-used // (rows * chips))
+    part = piece * chips
+    tiles = piece * rows * chips
+
+    def tile_buffer(*lead):
+        return pltpu.VMEM((*lead, SUB, WIDE), jnp.float32)
+
+    sems = [
+        pltpu.SemaphoreType.DMA((count,))
+        for count in (pairs_n, pairs_n, chips, chips, pairs_n, pairs_n)
+        for _ in range(2)
+    ]
+    return pl.pallas_call(
+        functools.partial(gram_kernel, (pairs_n, chips, piece)),
+        out_shape=jax.ShapeDtypeStruct((tiles, SUB, WIDE), jnp.float32),
+        in_specs=[pl.BlockSpec(memory_space=pltpu.VMEM)],
+        out_specs=pl.BlockSpec(memory_space=pltpu.VMEM),
+        scratch_shapes=[
+            tile_buffer(tiles),
+            tile_buffer(pairs_n, part),
+            tile_buffer(pairs_n, part),
+            tile_buffer(pairs_n, part),
+            tile_buffer(chips, piece),
+            tile_buffer(chips, piece),
+            *sems,
+            tile_buffer(tiles),
+        ],
+        compiler_params=pltpu.CompilerParams(
+            collective_id=0, has_side_effects=True, vmem_limit_bytes=40 * 2**20
+        ),
+    )(spectra)
+
+
 def factor_kernel(row_scale, gram, spectra, whitened, triangle, work, held):
-    n = gram.shape[0]
+    n = spectra.shape[1]
     blocks = n // WIDE
     groups = WIDE // SUB
 
     def at(i):
         return pl.ds(i * WIDE, WIDE)
 
+    place = {pair: k * groups for k, pair in enumerate(block_pairs(blocks))}
+
+    def block_of(p, q, r):
+        if p:
+            return work[at(q), at(r)]
+        first = place[q, r]
+        return gram[first : first + groups].reshape(WIDE, WIDE)
+
     for p in range(blocks):
-        source = gram if p == 0 else work
-        rows = [
-            source[p * WIDE + g * SUB : p * WIDE + (g + 1) * SUB, p * WIDE : (p + 1) * WIDE]
-            for g in range(groups)
-        ]
+        diagonal = block_of(p, p, p)
+        rows = [diagonal[g * SUB : (g + 1) * SUB] for g in range(groups)]
         upper, inverse = factor_block(rows)
         upper = jnp.concatenate(upper, axis=0)
         inverse = jnp.concatenate(inverse, axis=0)
@@ -111,16 +281,16 @@
             triangle[at(p), at(q)] = jnp.zeros((WIDE, WIDE), jnp.float32)
         right = []
         for q in range(p + 1, blocks):
-            block = mm(inverse, source[at(p), at(q)], ((1,), (0,)))
+            block = mm(inverse, block_of(p, p, q), ((1,), (0,)))
             right.append(block)
             triangle[at(p), at(q)] = block * (1.0 / row_scale)
             if q == p + 1:
-                work[at(q), at(q)] = source[at(q), at(q)] - mm(block, block, ((0,), (0,)))
+                work[at(q), at(q)] = block_of(p, q, q) - mm(block, block, ((0,), (0,)))
         for i, q in enumerate(range(p + 1, blocks)):
             for j, r in enumerate(range(p + 1, blocks)):
                 if r < q or (q == p + 1 and r == q):
                     continue
-                work[at(q), at(r)] = source[at(q), at(r)] - mm(right[i], right[j], ((0,), (0,)))
+                work[at(q), at(r)] = block_of(p, q, r) - mm(right[i], right[j], ((0,), (0,)))
         slab = spectra if p == 0 else held
         basis = mm(slab[:, at(p)], inverse, ((1,), (1,)))
         whitened[:, at(p)] = basis * row_scale
@@ -129,7 +299,7 @@
 
 
 def factor(gram, spectra, total_rows):
-    n = gram.shape[0]
+    n = spectra.shape[1]
     return pl.pallas_call(
         functools.partial(factor_kernel, math.sqrt(total_rows)),
         out_shape=(
@@ -146,13 +316,6 @@
     )(gram, spectra)
 
 
-def summed_gram(block):
-    gram = mm(block, block, ((0,), (0,)))
-    band = lax.psum_scatter(gram, "rows", scatter_dimension=0, tiled=True)
-    band = lax.psum(band, "chip")
-    return lax.all_gather(band, "rows", axis=0, tiled=True)
-
-
 def on_device(spectra):
     total_rows = lax.axis_size("rows") * lax.axis_size("chip") * spectra.shape[0]
     return factor(summed_gram(spectra), spectra, total_rows)

time: 133 us -> 40.6 us (0.31)
  waiting for transfers between devices: 102 us -> 0 us
  Pallas kernels: 12.9 us -> 38.7 us
  between operations: 13.7 us -> 0.65 us
  matrix products: 3.2 us -> 0 us
    reduce_scatter x1 -> x0, waiting for transfers between devices: 40 us -> none  [summed_gram(): band = lax.psum_scatter(gram, 'rows', scatter_dimension=0, tiled=True)]
    psum x1 -> x0, waiting for transfers between devices: 36.7 us -> none  [summed_gram(): band = lax.psum(band, 'chip')]
    pallas_call x0 -> x1, Pallas kernels: none -> 25.8 us  [summed_gram(): pl.pallas_call(functools.partial(gram_kernel, (pairs_n, chips, piece)), o...]
    all_gather x1 -> x0, waiting for transfers between devices: 25.2 us -> none  [summed_gram(): return lax.all_gather(band, 'rows', axis=0, tiled=True)]
    dot_general x1 -> x0, matrix products: 3.2 us -> none  [mm(): lax.dot_general(a, b, (dims, ((), ())), precision=HIGHEST, preferred_elem...]
  transfers between devices with their start and end apart: 3 -> 0, of which waited for: 3 -> 0; matrix products, arithmetic and copies ran while one was open for 0% -> 0% of each run, Pallas kernels for 0% -> 0%
where the time goes in v2:
time: 40.6 us; the launch traced here: 40.4 us
  Pallas kernels  38.7 us (95%)
  local copies, waits for them, and re-layouts  1.03 us (3%)
  between operations  0.65 us (2%)
    pallas_call x1, Pallas kernels, summed_gram(): pl.pallas_call(functools.partial(gram_kernel, (pairs_n, chips, piece)), o...  25.8 us
    pallas_call x1, Pallas kernels, factor(): pl.pallas_call(functools.partial(factor_kernel, math.sqrt(total_rows)), o...  12.9 us
    unnamed x2, local copies, waits for them, and re-layouts  1.03 us

profile of v2, /device:TPU:0, one launch (start us, length us, event | category | flops | bytes accessed | tf_op | source)
XLA Modules:
  0.0 40.4 jit_solution(12182638427665529837)
XLA Ops:
  0.6 0.0 copy-start
  0.6 1.0 %copy-done = f32[256,512]{1,0:T(8,128)S(1)} copy-done((f32[256,512]{1,0:T(8,128)S(1)}, f32[256,512]{1,0:T(8,128)}, u32[]{:S(2)}) %copy-start) | copy-done | bytes 524312
  1.7 25.8 %shard_map.30.gram = f32[160,8,128]{2,1,0:T(8,128)S(1)} custom-call(f32[256,512]{1,0:T(8,128)S(1)} %copy-done), custom_call_target="tpu_custom_call" | custom-call | tf_op jit(solution)/shard_map/pallas_call | solution.py:236
  27.5 12.9 %shard_map.31 = (f32[256,512]{1,0:T(8,128)}, f32[512,512]{1,0:T(8,128)}) custom-call(f32[160,8,128]{2,1,0:T(8,128)S(1)} %shard_map.30.gram, f32[256,512]{1,0:T(8,128)S(1)} %copy-done), custom_call_target="tpu_custom_call" | custom-call | tf_op jit(solution)/shard_map/pallas_call | solution.py:303
Async XLA Ops:
  0.6 1.0 %copy-start = (f32[256,512]{1,0:T(8,128)S(1)}, f32[256,512]{1,0:T(8,128)}, u32[]{:S(2)}) copy-start(f32[256,512]{1,0:T(8,128)} %spectra.3) | copy-start | bytes 1572868

commit v3 on v1

--- a/solution.py
+++ b/solution.py
@@ -27,7 +27,7 @@
     return jnp.broadcast_to(x[:, k : k + 1], (SUB, WIDE))
 
 
-def factor_block(groups):
+def factor_block(groups, tick):
     count = len(groups)
     groups = list(groups)
     sub = lax.broadcasted_iota(jnp.int32, (SUB, WIDE), 0)
@@ -35,6 +35,7 @@
     upper, inverse = [], []
     diag = [lane_of(groups[0], k) for k in range(SUB)]
     for g in range(count):
+        tick()
         p0 = g * SUB
         more = g + 1 < count
         own = (lane >= p0) & (lane < p0 + SUB)
@@ -89,73 +90,233 @@
     return upper, inverse
 
 
-def factor_kernel(row_scale, gram, spectra, whitened, triangle, work, held):
-    n = gram.shape[0]
+def chunk_blocks(blocks):
+    rows = [[(i, j) for j in range(i, blocks)] for i in range(blocks)]
+    chunks = [rows[0][:1], rows[0][1:], rows[1], sum(rows[2:], [])]
+    return [chunk for chunk in chunks if chunk]
+
+
+def chunk_sizes(n, row_count):
+    tiles = WIDE // SUB
+    return [-(-len(c) * tiles // row_count) for c in chunk_blocks(n // WIDE)]
+
+
+def sum_chunk(pairs_n, chips, part, blocks, slab, bufs, sems, started):
+    packed, from_pair, halves, from_hi, from_chip, gathered = bufs
+    send, recv = sems
+    half = pairs_n * part
+    row, chip = lax.axis_index("rows"), lax.axis_index("chip")
+    hi, lo = row // 2, row % 2
+    other = (hi * 2 + 1 - lo, chip)
+    tiles = WIDE // SUB
+    order = list(range(1, pairs_n)) + [0]
+
+    def hi_at(d):
+        return lax.rem(hi + d, pairs_n)
+
+    def remote(src, dst, slot, device):
+        copy = pltpu.make_async_remote_copy(
+            src_ref=src, dst_ref=dst, send_sem=send(slot), recv_sem=recv(slot),
+            device_id=device, device_id_type=pl.DeviceIdType.MESH,
+        )
+        copy.start()
+        started.append(copy)
+        return copy
+
+    slots = iter(range(4 * pairs_n + chips))
+    used = 0
+    for i, j in blocks:
+        left = slab[:, i * WIDE : (i + 1) * WIDE]
+        right = slab[:, j * WIDE : (j + 1) * WIDE]
+        packed[used : used + tiles] = mm(left, right, ((0,), (0,))).reshape(tiles, SUB, WIDE)
+        used += tiles
+    if used < 2 * half:
+        packed[used:] = jnp.zeros((2 * half - used, SUB, WIDE), jnp.float32)
+    yield
+    pair_copies = {}
+    for d in order:
+        source = packed.at[pl.ds((1 - lo) * half + hi_at(d) * part, part)]
+        pair_copies[d] = remote(source, from_pair.at[d], next(slots), other)
+    yield
+    copies = []
+    for d in order:
+        pair_copies[d].wait_recv()
+        mine = packed[pl.ds(lo * half + hi_at(d) * part, part)] + from_pair[d]
+        halves[d] = mine
+        if d:
+            device = (hi_at(d) * 2 + lo, chip)
+            copies.append(remote(halves.at[d], from_hi.at[d], next(slots), device))
+    yield
+    for copy in copies:
+        copy.wait_recv()
+    mine = halves[0]
+    for d in range(1, pairs_n):
+        mine = mine + from_hi[d]
+    from_chip[chip] = mine
+    spot = from_chip.at[chip]
+    copies = [
+        remote(spot, spot, next(slots), (row, lax.rem(chip + d, chips)))
+        for d in range(1, chips)
+    ]
+    yield
+    for copy in copies:
+        copy.wait_recv()
+    total = from_chip[0]
+    for c in range(1, chips):
+        total = total + from_chip[c]
+    own = pl.ds((lo * pairs_n + hi) * part, part)
+    gathered[own] = total
+    spot = gathered.at[own]
+    hi_copies = [
+        remote(spot, spot, next(slots), (hi_at(d) * 2 + lo, chip))
+        for d in range(1, pairs_n)
+    ]
+    copies = [remote(spot, spot, next(slots), other)]
+    yield
+    for d in range(1, pairs_n):
+        source = lax.rem(hi + pairs_n - d, pairs_n)
+        spot = gathered.at[pl.ds((lo * pairs_n + source) * part, part)]
+        hi_copies[d - 1].wait_recv()
+        copies.append(remote(spot, spot, next(slots), other))
+    yield
+    for copy in copies:
+        copy.wait_recv()
+
+
+BEFORE = (0, 1, 0, 2, 1, 0, 3, 2, 0, 1, 3, 0, 2, 0)
+DURING = (1, 3, 2, 1, 3, 1, 2, 2, 3, 3)
+
+
+def kernel(sizes, spectra, whitened, triangle, upper, held, send, recv, *bufs):
+    row_scale, pairs_n, chips, parts = sizes
+    n = spectra.shape[1]
     blocks = n // WIDE
     groups = WIDE // SUB
+    row, chip = lax.axis_index("rows"), lax.axis_index("chip")
+    hi, lo = row // 2, row % 2
 
     def at(i):
         return pl.ds(i * WIDE, WIDE)
 
+    barrier = pltpu.get_barrier_semaphore()
+    partners = [(hi * 2 + 1 - lo, chip)]
+    partners += [(lax.rem(hi + d, pairs_n) * 2 + lo, chip) for d in range(1, pairs_n)]
+    partners += [(row, lax.rem(chip + d, chips)) for d in range(1, chips)]
+    for device in partners:
+        pl.semaphore_signal(barrier, inc=1, device_id=device, device_id_type=pl.DeviceIdType.MESH)
+
+    started = []
+    chunks = chunk_blocks(blocks)
+    sums, place = [], {}
+    for c, (pairs, part) in enumerate(zip(chunks, parts)):
+        mine = bufs[6 * c : 6 * c + 6]
+        sems = (lambda s, c=c: send.at[c, s], lambda s, c=c: recv.at[c, s])
+        sums.append(sum_chunk(pairs_n, chips, part, pairs, spectra, mine, sems, started))
+        for k, pair in enumerate(pairs):
+            place[pair] = (mine[5], k * groups)
+    next(sums[0])
+    pl.semaphore_wait(barrier, len(partners))
+    next(sums[0])
+
+    def advance(c):
+        next(sums[c], None)
+
+    entered = {0}
+    for c in BEFORE[1:]:
+        if c not in entered:
+            entered.add(c)
+            advance(c)
+        advance(c)
+    todo = list(DURING)
+
+    def tick():
+        if todo:
+            advance(todo.pop(0))
+
+    def gram(q, r):
+        buf, first = place[q, r]
+        return buf[first : first + groups].reshape(WIDE, WIDE)
+
+    def less_above(p, q, r):
+        block = gram(q, r)
+        if p:
+            above = pl.ds(0, p * WIDE)
+            block = block - mm(upper[above, at(q)], upper[above, at(r)], ((0,), (0,)))
+        return block
+
+    diagonal = gram(0, 0)
+    slab = spectra[:, at(0)]
     for p in range(blocks):
-        source = gram if p == 0 else work
-        rows = [
-            source[p * WIDE + g * SUB : p * WIDE + (g + 1) * SUB, p * WIDE : (p + 1) * WIDE]
-            for g in range(groups)
-        ]
-        upper, inverse = factor_block(rows)
-        upper = jnp.concatenate(upper, axis=0)
+        rest = range(p + 1, blocks)
+        ahead = {q: less_above(p, p, q) for q in rest} if p else {}
+        corner = less_above(p, p + 1, p + 1) if p and rest else None
+        if p:
+            above = pl.ds(0, p * WIDE)
+            slab = spectra[:, at(p)] - mm(held[:, above], upper[above, at(p)], ((1,), (0,)))
+        rows = [diagonal[g * SUB : (g + 1) * SUB] for g in range(groups)]
+        own, inverse = factor_block(rows, tick)
+        while todo:
+            tick()
+        if p == 0:
+            ahead = {q: gram(0, q) for q in rest}
+            corner = gram(1, 1) if rest else None
         inverse = jnp.concatenate(inverse, axis=0)
-        triangle[at(p), at(p)] = upper * (1.0 / row_scale)
+        for q in rest:
+            block = mm(inverse, ahead[q], ((1,), (0,)))
+            upper[at(p), at(q)] = block
+            triangle[at(p), at(q)] = block * (1.0 / row_scale)
+            if q == p + 1:
+                diagonal = corner - mm(block, block, ((0,), (0,)))
+        triangle[at(p), at(p)] = jnp.concatenate(own, axis=0) * (1.0 / row_scale)
         for q in range(p):
             triangle[at(p), at(q)] = jnp.zeros((WIDE, WIDE), jnp.float32)
-        right = []
-        for q in range(p + 1, blocks):
-            block = mm(inverse, source[at(p), at(q)], ((1,), (0,)))
-            right.append(block)
-            triangle[at(p), at(q)] = block * (1.0 / row_scale)
-            if q == p + 1:
-                work[at(q), at(q)] = source[at(q), at(q)] - mm(block, block, ((0,), (0,)))
-        for i, q in enumerate(range(p + 1, blocks)):
-            for j, r in enumerate(range(p + 1, blocks)):
-                if r < q or (q == p + 1 and r == q):
-                    continue
-                work[at(q), at(r)] = source[at(q), at(r)] - mm(right[i], right[j], ((0,), (0,)))
-        slab = spectra if p == 0 else held
-        basis = mm(slab[:, at(p)], inverse, ((1,), (1,)))
+        basis = mm(slab, inverse, ((1,), (1,)))
+        held[:, at(p)] = basis
         whitened[:, at(p)] = basis * row_scale
-        for i, q in enumerate(range(p + 1, blocks)):
-            held[:, at(q)] = slab[:, at(q)] - mm(basis, right[i], ((1,), (0,)))
-
-
-def factor(gram, spectra, total_rows):
-    n = gram.shape[0]
+    for copy in started:
+        copy.wait_send()
+
+
+def on_device(spectra):
+    rows, chips = lax.axis_size("rows"), lax.axis_size("chip")
+    pairs_n = rows // 2
+    n = spectra.shape[1]
+    parts = chunk_sizes(n, rows)
+    row_scale = math.sqrt(rows * chips * spectra.shape[0])
+
+    def tiles(*lead):
+        return pltpu.VMEM((*lead, SUB, WIDE), jnp.float32)
+
+    bufs = []
+    for part in parts:
+        bufs += [
+            tiles(rows * part),
+            tiles(pairs_n, part),
+            tiles(pairs_n, part),
+            tiles(pairs_n, part),
+            tiles(chips, part),
+            tiles(rows * part),
+        ]
+    sems = pltpu.SemaphoreType.DMA((len(parts), 4 * pairs_n + chips))
     return pl.pallas_call(
-        functools.partial(factor_kernel, math.sqrt(total_rows)),
+        functools.partial(kernel, (row_scale, pairs_n, chips, parts)),
         out_shape=(
             jax.ShapeDtypeStruct(spectra.shape, jnp.float32),
             jax.ShapeDtypeStruct((n, n), jnp.float32),
         ),
-        in_specs=[pl.BlockSpec(memory_space=pltpu.VMEM)] * 2,
+        in_specs=[pl.BlockSpec(memory_space=pltpu.VMEM)],
         out_specs=(pl.BlockSpec(memory_space=pltpu.VMEM),) * 2,
         scratch_shapes=[
             pltpu.VMEM((n, n), jnp.float32),
             pltpu.VMEM(spectra.shape, jnp.float32),
+            sems,
+            sems,
+            *bufs,
         ],
-        compiler_params=pltpu.CompilerParams(vmem_limit_bytes=40 * 2**20),
-    )(gram, spectra)
-
-
-def summed_gram(block):
-    gram = mm(block, block, ((0,), (0,)))
-    band = lax.psum_scatter(gram, "rows", scatter_dimension=0, tiled=True)
-    band = lax.psum(band, "chip")
-    return lax.all_gather(band, "rows", axis=0, tiled=True)
-
-
-def on_device(spectra):
-    total_rows = lax.axis_size("rows") * lax.axis_size("chip") * spectra.shape[0]
-    return factor(summed_gram(spectra), spectra, total_rows)
+        compiler_params=pltpu.CompilerParams(
+            collective_id=0, has_side_effects=True, vmem_limit_bytes=40 * 2**20
+        ),
+    )(spectra)
 
 
 def solution(mesh):

time: 133 us -> 41.9 us (0.32)
  waiting for transfers between devices: 102 us -> 0 us
  Pallas kernels: 12.9 us -> 38.1 us
  between operations: 13.7 us -> 0.65 us
  matrix products: 3.2 us -> 0 us
  local copies, waits for them, and re-layouts: 1.23 us -> 2.8 us
    reduce_scatter x1 -> x0, waiting for transfers between devices: 40 us -> none  [summed_gram(): band = lax.psum_scatter(gram, 'rows', scatter_dimension=0, tiled=True)]
    psum x1 -> x0, waiting for transfers between devices: 36.7 us -> none  [summed_gram(): band = lax.psum(band, 'chip')]
    all_gather x1 -> x0, waiting for transfers between devices: 25.2 us -> none  [summed_gram(): return lax.all_gather(band, 'rows', axis=0, tiled=True)]
    pallas_call x1, Pallas kernels: 12.9 us -> 38.1 us  [on_device(): pl.pallas_call(functools.partial(kernel, (row_scale, pairs_n, chips, part...]
    dot_general x1 -> x0, matrix products: 3.2 us -> none  [mm(): lax.dot_general(a, b, (dims, ((), ())), precision=HIGHEST, preferred_elem...]
    unnamed x4, local copies, waits for them, and re-layouts: 1.23 us -> 2.8 us
  transfers between devices with their start and end apart: 3 -> 0, of which waited for: 3 -> 0; matrix products, arithmetic and copies ran while one was open for 0% -> 0% of each run, Pallas kernels for 0% -> 0%
where the time goes in v3:
time: 41.9 us; the launch traced here: 41.5 us
  Pallas kernels  38.1 us (91%)
  local copies, waits for them, and re-layouts  2.8 us (7%)
  between operations  0.65 us (2%)
    pallas_call x1, Pallas kernels, on_device(): pl.pallas_call(functools.partial(kernel, (row_scale, pairs_n, chips, part...  38.1 us
    unnamed x4, local copies, waits for them, and re-layouts  2.8 us

profile of v3, /device:TPU:0, one launch (start us, length us, event | category | flops | bytes accessed | tf_op | source)
XLA Modules:
  0.0 41.5 jit_solution(16480690099398435361)
XLA Ops:
  0.6 0.0 copy-start
  0.6 1.0 %copy-done = f32[256,512]{1,0:T(8,128)S(1)} copy-done((f32[256,512]{1,0:T(8,128)S(1)}, f32[256,512]{1,0:T(8,128)}, u32[]{:S(2)}) %copy-start) | copy-done | bytes 524312
  1.7 38.1 %shard_map.30 = (f32[256,512]{1,0:T(8,128)S(1)}, f32[512,512]{1,0:T(8,128)S(1)}) custom-call(f32[256,512]{1,0:T(8,128)S(1)} %copy-done), custom_call_target="tpu_custom_call" | custom-call | tf_op jit(solution)/shard_map/pallas_call | solution.py:301
  39.8 0.8 %copy.5 = f32[256,512]{1,0:T(8,128)} copy(f32[256,512]{1,0:T(8,128)S(1)} %get-tuple-element.4) | data formatting | bytes 1048576
  40.6 1.0 %copy.6 = f32[512,512]{1,0:T(8,128)} copy(f32[512,512]{1,0:T(8,128)S(1)} %get-tuple-element.5) | data formatting | bytes 2097152
Async XLA Ops:
  0.6 1.0 %copy-start = (f32[256,512]{1,0:T(8,128)S(1)}, f32[256,512]{1,0:T(8,128)}, u32[]{:S(2)}) copy-start(f32[256,512]{1,0:T(8,128)} %spectra.1) | copy-start | bytes 1572868
